TPU v7x, 768 devices: a whole 4x8x12 slice. The times are simulated.
768 devices in a mesh: rep: 96 (over x, z, core), leaf: 8 (over y).
Axes of the slice: x: 4, y: 8, z: 12, core: 2. Of those that a mesh axis runs over, the one named last changes fastest.
Arguments:
- grads: bfloat16 [96, 8, 64, 24576], P('rep', 'leaf'), may hold values from -6 to 6
- momentum: float32 [96, 64, 24576], P('rep', None, 'leaf'), may hold values from -6 to 6
- picks: int32 [96, 1, 384, 32], P('rep', None, 'leaf'), may hold values from 0 to 4095, as said below
- counts: int32 [96, 1, 384], P('rep', None, 'leaf'), may hold values from 1 to 32, as said below
Outputs:
- new_momentum: float32 [96, 64, 24576], P('rep', None, 'leaf')
- update: bfloat16 [64, 24576], replicated
Inputs may be any that keep to these rules, and one draw needn't show every extreme that they name: `picks`: within one block of one replica the 32 indices are distinct, padding slots included. `counts`: every replica has a block with all 32 slots used.
All inputs are finite; a program needn't handle non-finite values.
Results may differ from a plain program's by a relative error of at most 0.02.
Values may be sent and summed in bfloat16 or wider, within the bound.
No kernel may reach another device: no remote copies, remote signals or barrier semaphores. Data moves between devices by JAX's collectives and lax.ppermute only.
A program may use at most 64 MiB of HBM per device.

v0:
```python
import functools

import jax
import jax.numpy as jnp
import numpy as np
from jax import lax
from jax.experimental import pallas as pl
from jax.experimental.pallas import tpu as pltpu
from jax.sharding import Mesh, PartitionSpec as P

SPAN = 64
LANES = 128
QUAD = 4 * SPAN
NX, NC = 4, 2
F32, BF16 = jnp.float32, jnp.bfloat16
VMEM_LIMIT = 24 * 1024 * 1024


def split(a):
    hi = a.astype(BF16)
    return hi, (a - hi.astype(F32)).astype(BF16)


def tables():
    f = np.arange(SPAN)[:, None]
    i = np.arange(SPAN)[None, :]
    scale = np.where(f == 0, np.sqrt(1.0 / SPAN), np.sqrt(2.0 / SPAN))
    c = (scale * np.cos(np.pi * (2 * i + 1) * f / (2 * SPAN))).astype(np.float32)
    return c


def two_parts(c):
    hi = c.astype(jnp.bfloat16)
    lo = (c - hi.astype(np.float32)).astype(jnp.bfloat16)
    return hi, lo


def dot(a, b):
    return lax.dot_general(a, b, (((1,), (0,)), ((), ())), preferred_element_type=F32)


def dot_t(a, b):
    return lax.dot_general(a, b, (((1,), (1,)), ((), ())), preferred_element_type=F32)


def quads(x):
    n = x.shape[1] // QUAD
    return jnp.concatenate([x[:, QUAD * a : QUAD * (a + 1)] for a in range(n)], axis=0)


def lane_iota(shape):
    return lax.broadcasted_iota(jnp.int32, shape, len(shape) - 1)


def column_transform(x32, wide, hi_only):
    hi, lo = split(x32)
    both = dot(hi, wide)
    return both[:, :QUAD] + both[:, QUAD:] + dot(lo, hi_only)


def frequencies(ids):
    known = jnp.maximum(ids, 0)
    return lax.shift_right_logical(known, 6), jnp.bitwise_and(known, SPAN - 1)


def picked(f, ids, rows):
    lane = lane_iota((SPAN, LANES))
    _, v = frequencies(ids)
    at = jnp.broadcast_to(v, (SPAN, LANES)) + jnp.bitwise_and(lax.shift_left(lane, 1), SPAN)
    left = jnp.take_along_axis(f[:, :LANES], at, axis=1, mode="promise_in_bounds")
    right = jnp.take_along_axis(f[:, LANES:], at, axis=1, mode="promise_in_bounds")
    value = jnp.sum(jnp.where(lane < SPAN, left, right) * rows, axis=0, keepdims=True)
    return jnp.where(ids >= 0, value, 0.0)


def fetch(pairs, sems):
    copies = [pltpu.make_async_copy(src, dst, sems.at[i]) for i, (src, dst) in enumerate(pairs)]
    for copy in copies:
        copy.start()
    return copies


def ids_kernel(picks_hbm, counts_hbm, out_ref, picks_ref, counts_ref, sems):
    for copy in fetch([(picks_hbm, picks_ref), (counts_hbm, counts_ref)], sems):
        copy.wait()
    slots, n = picks_ref.shape
    slot = lax.broadcasted_iota(jnp.int32, (slots, n), 0)
    ids = jnp.where(slot < counts_ref[...], picks_ref[...], -1).T
    rows = n // 4
    lines = [
        jnp.concatenate([ids[4 * a + g : 4 * a + g + 1, :] for g in range(4)], axis=1)
        for a in range(rows)
    ]
    lines.append(jnp.full((out_ref.shape[1] - rows, LANES), -1, jnp.int32))
    full = jnp.concatenate(lines, axis=0)
    for y in range(out_ref.shape[0]):
        out_ref[y] = full


def dense_kernel(
    leaves, me_ref, g_hbm, m_hbm, wide_hbm, f_hbm, buf, m_ref, wide_ref, f_ref, sems, outs
):
    cols = g_hbm.shape[1] // leaves
    pairs = [(wide_hbm, wide_ref)]
    pairs += [(g_hbm.at[:, y * cols : (y + 1) * cols], buf.at[y]) for y in range(leaves)]
    pairs += [(m_hbm, m_ref)]
    copies = fetch(pairs, sems)
    copies[0].wait()
    me = me_ref[0]
    back = []
    for y in range(leaves):
        copies[1 + y].wait()
        both = dot(quads(buf[y]), wide_ref[...])
        f_ref[y] = both[:, :QUAD] + both[:, QUAD:]
        if y == 0:
            copies[leaves + 1].wait()

        @pl.when(me == y)
        def _():
            own = column_transform(quads(0.9 * m_ref[...]), wide_ref[...], wide_ref[:, :QUAD])
            f_ref[y] += own

        copy = pltpu.make_async_copy(f_ref.at[y], f_hbm.at[y], outs.at[y])
        copy.start()
        back.append(copy)
    for copy in back:
        copy.wait()


def coeff_kernel(rows, f_hbm, ids_hbm, tab_hbm, out_ref, f_ref, ids_ref, tab_ref, sems):
    leaves = f_hbm.shape[0]
    pairs = [(ids_hbm, ids_ref), (tab_hbm, tab_ref)]
    first, second, *copies = fetch(pairs + [(f_hbm.at[y], f_ref.at[y]) for y in range(leaves)], sems)
    first.wait()
    second.wait()
    both = jnp.concatenate([tab_ref[2], tab_ref[3]], axis=0)
    short = lax.broadcasted_iota(jnp.int32, (SPAN, LANES), 0)
    for y in range(leaves):
        lines = [ids_ref[y, a : a + 1, :] for a in range(rows)]
        hot = [jnp.where(short == frequencies(ids)[0], 1.0, 0.0).astype(BF16) for ids in lines]
        table = dot(both, jnp.concatenate(hot, axis=1))
        table = table[:SPAN] + table[SPAN:]
        copies[y].wait()
        for a in range(rows):
            f = f_ref[y, SPAN * a : SPAN * (a + 1), :]
            out_ref[y, a : a + 1, :] = picked(f, lines[a], table[:, LANES * a : LANES * (a + 1)])
        out_ref[y, rows:, :] = jnp.zeros((out_ref.shape[1] - rows, LANES), F32)


def regroup_kernel(per, got_ref, ids_ref, out_ref):
    total = got_ref[0]
    for l in range(1, got_ref.shape[0]):
        total = total + got_ref[l]
    total = total.astype(BF16).astype(F32)
    ids = jnp.maximum(ids_ref[0], 0).astype(F32)
    low = lane_iota((1, LANES)) < SPAN
    for x in range(NX):
        for c in range(NC):
            keep = low if c == 0 else jnp.logical_not(low)
            full, half = per * x + (per - 1) * c, per * x + 1
            value, index = total[half : half + 1], ids[half : half + 1]
            mixed = jnp.where(keep, value, pltpu.roll(index, SPAN, 1))
            page = jnp.concatenate([total[full : full + 1], mixed, ids[full : full + 1]], axis=1)
            for z in range(out_ref.shape[1]):
                out_ref[x, z, c] = page


def update_kernel(per, core_ref, got_ref, tab_hbm, out_ref, tab_ref, sems):
    (copy,) = fetch([(tab_hbm, tab_ref)], sems)
    peers = got_ref.shape[0]
    tall = lax.broadcasted_iota(jnp.int32, (2 * SPAN, LANES), 0)
    short = lax.broadcasted_iota(jnp.int32, (SPAN, LANES), 0)
    block = lax.shift_left(jnp.bitwise_and(lax.shift_right_logical(lane_iota((1, LANES)), 5), 1), 6)
    low = lane_iota((1, LANES)) < SPAN
    first_core = core_ref[0] == 0

    def two_peers(n):
        a, b = got_ref[n], got_ref[n + 1]
        mixed_a, mixed_b = a[:, LANES : 2 * LANES], b[:, LANES : 2 * LANES]
        turned_a, turned_b = pltpu.roll(mixed_a, SPAN, 1), pltpu.roll(mixed_b, SPAN, 1)
        firsts, seconds = [], []
        for at in (0, 2 * LANES):
            one, two = a[:, at : at + LANES], b[:, at : at + LANES]
            firsts.append(jnp.where(low, one, pltpu.roll(two, SPAN, 1)))
            seconds.append(jnp.where(low, pltpu.roll(one, SPAN, 1), two))
        here = jnp.where(low, mixed_a, turned_b)
        there = jnp.where(low, turned_a, mixed_b)
        value = jnp.where(first_core, here, there)
        index = jnp.where(first_core, there, here)
        return firsts, seconds, (value, index)

    def four_peers(n, sums):
        pairs = [two_peers(4 * n), two_peers(4 * n + 2)]
        new = []
        for a in range(per):
            left, right = [], []
            for lines in pairs:
                value, ids = lines[a][0], lines[a][1].astype(jnp.int32)
                u = lax.shift_right_logical(ids, 6) + block
                v = jnp.bitwise_and(ids, SPAN - 1)
                left.append(jnp.where(tall == u, value, 0.0).astype(BF16))
                right.append(jnp.where(short == v, 1.0, 0.0).astype(BF16))
            new.append(
                sums[a] + dot_t(jnp.concatenate(left, axis=1), jnp.concatenate(right, axis=1))
            )
        return tuple(new)

    zero = jnp.zeros((2 * SPAN, SPAN), F32)
    sums = lax.fori_loop(0, peers // 4, four_peers, (zero,) * per, unroll=True)
    z = jnp.concatenate(sums, axis=0)
    z_hi, z_lo = split(z)
    copy.wait()
    c_hi, c_lo, ct_hi, ct_lo = [tab_ref[i] for i in range(4)]
    w = dot(z_hi, c_hi) + (dot(z_hi, c_lo) + dot(z_lo, c_hi))
    flat = jnp.concatenate([w[SPAN * b : SPAN * (b + 1)] for b in range(2 * per)], axis=1)
    w_hi, w_lo = split(flat)
    field = dot(ct_hi, w_hi) + (dot(ct_lo, w_hi) + dot(ct_hi, w_lo))
    edge = 2 * LANES
    turned = jnp.concatenate([field[:, edge:], field[:, :edge]], axis=1)
    field = jnp.where(core_ref[0] == 0, field, turned).astype(BF16)
    for y in range(out_ref.shape[0]):
        out_ref[y] = field


def residual_kernel(step, sum_ref, m_ref, ids_ref, wide_ref, ct_ref, out_ref):
    first = pl.program_id(0) * step
    x = 0.9 * m_ref[...] + sum_ref[...].astype(F32)
    f = column_transform(quads(x), wide_ref[...], wide_ref[:, :QUAD])
    ct = ct_ref[...]
    group = lax.shift_right_logical(lane_iota((SPAN, LANES)), 5)
    for a in range(step):
        ids = ids_ref[0, pl.ds(first + a, 1), :]
        u, v = [jnp.broadcast_to(w, (SPAN, LANES)) for w in frequencies(ids)]
        rows = jnp.take_along_axis(ct, u, axis=1, mode="promise_in_bounds")
        cols = jnp.take_along_axis(ct, v, axis=1, mode="promise_in_bounds")
        value = picked(f[SPAN * a : SPAN * (a + 1)], ids, rows)
        cols = jnp.concatenate([jnp.where(group == b, cols, 0.0) for b in range(4)], axis=0)
        l_hi, l_lo = split(rows * value)
        r_hi, r_lo = split(cols)
        taken = dot_t(l_hi, r_hi) + (dot_t(l_hi, r_lo) + dot_t(l_lo, r_hi))
        out_ref[:, QUAD * a : QUAD * (a + 1)] = x[:, QUAD * a : QUAD * (a + 1)] - taken


def place_kernel(own, others, x_ref, core_ref, *refs):
    out_hbm, sem = refs[-2], refs[-1]
    x, core = x_ref[0], core_ref[0]
    pieces, at = [], []
    for hops, c, ref in zip(own + others, [core] * len(own) + [1 - core] * len(others), refs):
        several = hops if isinstance(hops, tuple) else (hops,)
        pieces += [ref.at[i] for i in range(len(several))] if hops is several else [ref]
        at += [jnp.bitwise_and(x + (NX - n), NX - 1) * NC + c for n in several]
    leaves, _, cols = pieces[0].shape
    copies = []
    for i, piece in enumerate(pieces):
        for y in range(leaves):
            to = pl.multiple_of((y * NX * NC + at[i]) * cols, LANES)
            copies.append(
                pltpu.make_async_copy(piece.at[y], out_hbm.at[:, pl.ds(to, cols)], sem.at[len(copies)])
            )
    for copy in copies:
        copy.start()
    for copy in copies:
        copy.wait()


def call(kernel, out_shape, vmem=VMEM_LIMIT, **kw):
    return pl.pallas_call(
        kernel,
        out_shape=out_shape,
        compiler_params=pltpu.CompilerParams(vmem_limit_bytes=vmem),
        **kw,
    )


def on_device(nz, leaves, grads, momentum, picks, counts):
    c = tables()
    c_hi, c_lo = two_parts(c)
    ct_hi, ct_lo = two_parts(np.ascontiguousarray(c.T))
    eye = np.eye(4, dtype=np.float32)
    bd_hi = np.kron(eye, ct_hi.astype(np.float32)).astype(jnp.bfloat16)
    bd_lo = np.kron(eye, ct_lo.astype(np.float32)).astype(jnp.bfloat16)
    wide = jnp.asarray(np.concatenate([bd_hi, bd_lo], axis=1))
    tab = jnp.asarray(np.stack([c_hi, c_lo, ct_hi, ct_lo]))
    ct = jnp.asarray(np.concatenate([c.T, c.T], axis=1))

    columns = grads.shape[3]
    own_cols = columns // leaves
    blocks, slots = picks.shape[2:]
    rows = blocks // 4
    per = rows // NX
    peers = nz * NC
    g = grads.reshape(SPAN, columns)
    m = momentum.reshape(SPAN, own_cols)
    leaf = lax.axis_index("leaf")
    core = lax.axis_index("core")
    whole = pl.BlockSpec(memory_space=pltpu.VMEM)
    scalar = pl.BlockSpec(memory_space=pltpu.SMEM)
    hbm = pl.BlockSpec(memory_space=pltpu.HBM)
    anywhere = pl.BlockSpec(memory_space=pl.ANY)
    dma = pltpu.SemaphoreType.DMA

    summed = lax.psum_scatter(g, "leaf", scatter_dimension=1, tiled=True)

    own_ids = call(
        ids_kernel,
        jax.ShapeDtypeStruct((leaves, 16, LANES), jnp.int32),
        vmem=62 * 1024 * 1024,
        in_specs=[hbm, hbm],
        scratch_shapes=[
            pltpu.VMEM((slots, blocks), jnp.int32),
            pltpu.VMEM((1, blocks), jnp.int32),
            dma((2,)),
        ],
    )(picks.reshape(blocks, slots).T, counts.reshape(1, blocks))
    all_ids = lax.all_to_all(own_ids, "leaf", 0, 0, tiled=True)

    f = call(
        functools.partial(dense_kernel, leaves),
        jax.ShapeDtypeStruct((leaves, rows * SPAN, QUAD), F32),
        vmem=56 * 1024 * 1024,
        in_specs=[scalar, hbm, hbm, hbm],
        out_specs=hbm,
        scratch_shapes=[
            pltpu.VMEM((leaves, SPAN, own_cols), BF16),
            pltpu.VMEM((SPAN, own_cols), F32),
            pltpu.VMEM(wide.shape, BF16),
            pltpu.VMEM((leaves, rows * SPAN, QUAD), F32),
            dma((leaves + 2,)),
            dma((leaves,)),
        ],
        cost_estimate=pl.CostEstimate(flops=2 * 10**9, bytes_accessed=16 * 10**6, transcendentals=0),
    )(leaf.reshape(1), g, m, wide)

    partial = call(
        functools.partial(coeff_kernel, rows),
        jax.ShapeDtypeStruct((leaves, 16, LANES), F32),
        vmem=50 * 1024 * 1024,
        in_specs=[hbm, anywhere, hbm],
        scratch_shapes=[
            pltpu.VMEM((leaves, rows * SPAN, QUAD), F32),
            pltpu.VMEM(all_ids.shape, jnp.int32),
            pltpu.VMEM(tab.shape, BF16),
            dma((leaves + 2,)),
        ],
    )(f, all_ids, tab)
    got = lax.all_to_all(partial, "leaf", 0, 0, tiled=True)

    sent = call(
        functools.partial(regroup_kernel, per),
        jax.ShapeDtypeStruct((NX, nz, NC, 1, 3 * LANES), F32),
    )(got, own_ids)
    got = lax.all_to_all(
        sent.reshape(NX * peers, 1, 3 * LANES), ("x", "z", "core"), 0, 0, tiled=True
    )

    wide_cols = 2 * per * SPAN
    field = call(
        functools.partial(update_kernel, per),
        jax.ShapeDtypeStruct((leaves, SPAN, wide_cols), BF16),
        in_specs=[scalar, whole, hbm],
        scratch_shapes=[pltpu.VMEM(tab.shape, BF16), dma((1,))],
    )(core.reshape(1), got, tab)
    summed, field = lax.optimization_barrier((summed, field))
    field = lax.all_to_all(field, "leaf", 0, 0, tiled=True)

    def along_x(hops):
        return lax.ppermute(field, "x", [(i, (i + hops) % NX) for i in range(NX)])

    def across(a):
        return lax.ppermute(a, "core", [(0, 1), (1, 0)])

    mine = {hops: along_x(hops) for hops in (2, 1, 3)}

    step = 3
    residual = call(
        functools.partial(residual_kernel, step),
        jax.ShapeDtypeStruct((SPAN, own_cols), F32),
        grid=(rows // step,),
        in_specs=[
            pl.BlockSpec((SPAN, step * QUAD), lambda i: (0, i)),
            pl.BlockSpec((SPAN, step * QUAD), lambda i: (0, i)),
            pl.BlockSpec((1, 16, LANES), lambda i: (0, 0, 0)),
            whole,
            whole,
        ],
        out_specs=pl.BlockSpec((SPAN, step * QUAD), lambda i: (0, i)),
        cost_estimate=pl.CostEstimate(flops=10**9, bytes_accessed=16 * 10**6, transcendentals=0),
    )(summed, m, own_ids, wide, ct)

    residual, mine[2] = lax.optimization_barrier((residual, mine[2]))
    beside, beside_far = across(field), across(mine[2])
    order = (1, 3)
    rest = jnp.stack([mine[hops] for hops in order])
    beside, beside_far, rest = lax.optimization_barrier((beside, beside_far, rest))
    x = lax.axis_index("x")

    def place(own, others, base):
        pieces = [*own.values(), *others.values()]
        last = () if base is None else (base,)
        return call(
            functools.partial(place_kernel, list(own), list(others)),
            jax.ShapeDtypeStruct((SPAN, columns), BF16),
            in_specs=[scalar] * 2 + [anywhere] * (len(pieces) + len(last)),
            out_specs=hbm,
            scratch_shapes=[dma((NX * NC * leaves,))],
            input_output_aliases={} if base is None else {len(pieces) + 2: 0},
            cost_estimate=pl.CostEstimate(flops=0, bytes_accessed=4 * 10**6, transcendentals=0),
        )(x.reshape(1), core.reshape(1), *pieces, *last)

    update = place({0: field, 2: mine[2], order: rest}, {0: beside, 2: beside_far}, None)
    update = place({}, {order: across(rest)}, update)
    return (residual[None], update)


def solution(mesh):
    reps, leaves = mesh.devices.shape
    nz = reps // (NX * NC)
    fine = Mesh(mesh.devices.reshape(NX, nz, NC, leaves), ("x", "z", "core", "leaf"))
    rep = ("x", "z", "core")
    placed = (
        P(rep, "leaf", None, None),
        P(rep, None, "leaf"),
        P(rep, None, "leaf", None),
        P(rep, None, "leaf"),
    )
    return jax.shard_map(
        functools.partial(on_device, nz, leaves),
        mesh=fine,
        in_specs=placed,
        out_specs=(P(rep, None, "leaf"), P()),
        check_vma=False,
    )
```

profile of v0, /device:TPU:1, one launch (start us, length us, event | category | flops | bytes accessed | tf_op | source)
XLA Modules:
  0.0 132.9 jit_solution(9824124159223947192)
XLA Ops:
  7.2 0.0 reduce-scatter.2.cloned.1.call-start
  7.2 0.7 reduce-scatter.2.cloned.1.call-update
  7.9 1.5 %shard_map.87.ids_ref = s32[8,16,128]{2,1,0:T(8,128)} custom-call(s32[32,48]{1,0:T(8,128)} %bitcast.19, s32[1,48]{1,0:T(1,128)} %bitcast.20), custom_call_target="tpu_custom_call" | custom-call | tf_op jit(solution)/shard_map/pallas_call | solution.py:304
  9.4 7.7 %all-to-all-start = ((s32[8,16,128]{2,1,0:T(8,128)}), s32[8,16,128]{2,1,0:T(8,128)S(1)}, u32[]{:S(2)}, u32[]{:S(2)}) async-start(s32[8,16,128]{2,1,0:T(8,128)} %shard_map.87.ids_ref), calls=%async_computation.1 | async-start | bytes 131072 | tf_op jit(solution)/shard_map/all_to_all | solution.py:315
  17.1 0.0 copy-start.2
  17.1 6.3 %shard_map.86.f_hbm = f32[8,768,256]{2,1,0:T(8,128)} custom-call(s32[1]{0:T(128)} %bitcast.2.me_ref, bf16[64,24576]{1,0:T(8,128)(2,1)} %bitcast.16, f32[64,3072]{1,0:T(8,128)} %bitcast.13, bf16[256,512]{1,0:T(8,128)(2,1)} %constant.19.clone.wide_hbm.wide_ref), custom_call_target="tpu_custom_call" | custom-call | flops 2000000000 | bytes 16000000 | tf_op jit(solution)/shard_map/pallas_call | solution.py:317
  23.4 0.0 copy-start.1
  23.4 0.0 copy-start
  23.4 0.0 copy-start.3
  23.4 0.0 copy-start.5
  23.4 0.9 all-to-all-done.ids_hbm
  24.3 0.0 copy-done.2
  24.3 4.3 %shard_map.88 = f32[8,16,128]{2,1,0:T(8,128)S(1)} custom-call(f32[8,768,256]{2,1,0:T(8,128)} %shard_map.86.f_hbm, s32[8,16,128]{2,1,0:T(8,128)S(1)} %all-to-all-done.ids_hbm, bf16[4,64,64]{2,1,0:T(8,128)(2,1)S(1)} %copy-done.2), custom_call_target="tpu_custom_call" | custom-call | tf_op jit(solution)/shard_map/pallas_call | solution.py:334
  28.6 13.3 %all_to_all.20.got_ref = f32[8,16,128]{2,1,0:T(8,128)S(1)} all-to-all(f32[8,16,128]{2,1,0:T(8,128)S(1)} %shard_map.88), channel_id=1, replica_groups=mesh['x'=4,'z'=12,'core'=2,'leaf'=8] {'leaf'}, dimensions={0} | all-to-all | bytes 131072 | tf_op jit(solution)/shard_map/all_to_all | solution.py:346
  42.0 0.0 copy-done.1
  42.0 0.8 shard_map.89
  42.7 21.7 %all-to-all-start.2 = ((f32[96,1,384]{2,1,0:T(1,128)}), f32[96,1,384]{2,1,0:T(1,128)S(1)}, u32[]{:S(2)}, u32[]{:S(2)}) async-start(f32[96,1,384]{2,1,0:T(1,128)} %bitcast.7), calls=%async_computation.3 | async-start | bytes 294912 | tf_op jit(solution)/shard_map/all_to_all | solution.py:352
  64.4 14.6 %all-to-all-done.2.got_ref = f32[96,1,384]{2,1,0:T(1,128)S(1)} async-done(((f32[96,1,384]{2,1,0:T(1,128)}), f32[96,1,384]{2,1,0:T(1,128)S(1)}, u32[]{:S(2)}, u32[]{:S(2)}) %all-to-all-start.2) | async-done | bytes 147488 | tf_op jit(solution)/shard_map/all_to_all | solution.py:352
  79.0 2.2 %shard_map.90 = bf16[8,64,384]{2,1,0:T(8,128)(2,1)S(1)} custom-call(s32[1]{0:T(128)} %bitcast.1.core_ref, f32[96,1,384]{2,1,0:T(1,128)S(1)} %all-to-all-done.2.got_ref, bf16[4,64,64]{2,1,0:T(8,128)(2,1)S(1)} %copy-done.2), custom_call_target="tpu_custom_call" | custom-call | tf_op jit(solution)/shard_map/pallas_call | solution.py:357
  81.2 0.0 reduce-scatter.2.cloned.1.call-done.sum_ref
  81.2 15.4 %all_to_all.21.refs_0_ = bf16[8,64,384]{2,1,0:T(8,128)(2,1)S(1)} all-to-all(bf16[8,64,384]{2,1,0:T(8,128)(2,1)S(1)} %shard_map.90), channel_id=1, replica_groups=mesh['x'=4,'z'=12,'core'=2,'leaf'=8] {'leaf'}, dimensions={0} | all-to-all | bytes 786432 | tf_op jit(solution)/shard_map/all_to_all | solution.py:364
  96.7 2.8 %collective-permute-start = (bf16[8,64,384]{2,1,0:T(8,128)(2,1)S(1)}, bf16[8,64,384]{2,1,0:T(8,128)(2,1)S(1)}, u32[]{:S(2)}, u32[]{:S(2)}) collective-permute-start(bf16[8,64,384]{2,1,0:T(8,128)(2,1)S(1)} %all_to_all.21.refs_0_), channel_id=1, source_target_pairs={{0,384},{192,576},{384,0},{576,192},{1,385},{193,577},{385,1},{577... | collective-permute-start | bytes 1179656 | tf_op jit(solution)/shard_map/ppermute | solution.py:367
  99.5 3.9 %collective-permute-start.4 = (bf16[8,64,384]{2,1,0:T(8,128)(2,1)S(1)}, bf16[8,64,384]{2,1,0:T(8,128)(2,1)S(1)}, u32[]{:S(2)}, u32[]{:S(2)}) collective-permute-start(bf16[8,64,384]{2,1,0:T(8,128)(2,1)S(1)} %all_to_all.21.refs_0_), channel_id=1, source_target_pairs={{0,576},{192,0},{384,192},{576,384},{1,577},{193,1},{385,193},{577... | collective-permute-start | bytes 1179656 | tf_op jit(solution)/shard_map/ppermute | solution.py:367
  103.3 1.9 %collective-permute-start.3 = (bf16[8,64,384]{2,1,0:T(8,128)(2,1)S(1)}, bf16[8,64,384]{2,1,0:T(8,128)(2,1)S(1)}, u32[]{:S(2)}, u32[]{:S(2)}) collective-permute-start(bf16[8,64,384]{2,1,0:T(8,128)(2,1)S(1)} %all_to_all.21.refs_0_), channel_id=1, source_target_pairs={{0,192},{192,384},{384,576},{576,0},{1,193},{193,385},{385,577},{5... | collective-permute-start | bytes 1179656 | tf_op jit(solution)/shard_map/ppermute | solution.py:367
  105.3 0.0 copy-done
  105.3 0.0 copy-done.3
  105.3 0.0 copy-done.5
  105.3 0.0 copy-start.4
  105.3 1.0 copy-done.4
  106.3 3.7 %shard_map.91 = f32[64,3072]{1,0:T(8,128)} custom-call(bf16[64,3072]{1,0:T(8,128)(2,1)S(1)} %copy-done.4, f32[64,3072]{1,0:T(8,128)S(1)} %bitcast.14, s32[8,16,128]{2,1,0:T(8,128)S(1)} %copy-done.1, bf16[256,512]{1,0:T(8,128)(2,1)S(1)} %copy-done.3, f32[64,128]{1,0:T(8,128)S(1)} %copy-done.5), custom_call_target="tpu_custom_call" | custom-call | flops 1000000000 | bytes 16000000 | tf_op jit(solution)/shard_map/pallas_call | solution.py:375
  110.0 5.1 %collective-permute-start.1 = (bf16[8,64,384]{2,1,0:T(8,128)(2,1)S(1)}, bf16[8,64,384]{2,1,0:T(8,128)(2,1)S(1)}, u32[]{:S(2)}, u32[]{:S(2)}) collective-permute-start(bf16[8,64,384]{2,1,0:T(8,128)(2,1)S(1)} %all_to_all.21.refs_0_), channel_id=1, source_target_pairs={{0,8},{8,0},{1,9},{9,1},{2,10},{10,2},{3,11},{11,3},{4,12},{12,4},... | collective-permute-start | bytes 1179656 | tf_op jit(solution)/shard_map/ppermute | solution.py:370
  115.1 0.0 collective-permute-done.refs_1_
  115.1 1.9 %collective-permute-start.2 = (bf16[8,64,384]{2,1,0:T(8,128)(2,1)S(1)}, bf16[8,64,384]{2,1,0:T(8,128)(2,1)S(1)}, u32[]{:S(2)}, u32[]{:S(2)}) collective-permute-start(bf16[8,64,384]{2,1,0:T(8,128)(2,1)S(1)} %collective-permute-done.refs_1_), channel_id=1, source_target_pairs={{0,8},{8,0},{1,9},{9,1},{2,10},{10,2},{3,11},{11,3},{4,12},{12,4},... | collective-permute-start | bytes 1179656 | tf_op jit(solution)/shard_map/ppermute | solution.py:370
  117.0 0.0 collective-permute-done.4
  117.0 1.3 collective-permute-done.3
  118.3 0.1 pad_maximum_fusion.refs_2_
  118.4 0.0 collective-permute-done.1.refs_3_
  118.4 0.3 collective-permute-done.2.refs_4_
  118.7 3.9 %collective-permute-start.5 = (bf16[2,8,64,384]{3,2,1,0:T(8,128)(2,1)S(1)}, bf16[2,8,64,384]{3,2,1,0:T(8,128)(2,1)S(1)}, u32[]{:S(2)}, u32[]{:S(2)}) collective-permute-start(bf16[2,8,64,384]{3,2,1,0:T(8,128)(2,1)S(1)} %pad_maximum_fusion.refs_2_), channel_id=1, source_target_pairs={{0,8},{8,0},{1,9},{9,1},{2,10},{10,2},{3,11},{11,3},{4,12},{12,4},... | collective-permute-start | bytes 2359304 | tf_op jit(solution)/shard_map/ppermute | solution.py:370
  122.6 1.9 %shard_map.92.refs_1_ = bf16[64,24576]{1,0:T(8,128)(2,1)} custom-call(s32[1]{0:T(128)} %bitcast.9.x_ref, s32[1]{0:T(128)} %bitcast.1.core_ref, bf16[8,64,384]{2,1,0:T(8,128)(2,1)S(1)} %all_to_all.21.refs_0_, bf16[8,64,384]{2,1,0:T(8,128)(2,1)S(1)} %collective-permute-done.refs_1_, bf16[2,8,64,384]{3,2,1,0:T(8,128)(2,1)S(1)} %pad_maximum_fusion.refs_2_, ...), custom_call_target="tpu_custom_call" | custom-call | bytes 4000000 | tf_op jit(solution)/shard_map/pallas_call | solution.py:400
  124.5 0.0 collective-permute-done.5.refs_0_
  124.6 1.4 %shard_map.93 = bf16[64,24576]{1,0:T(8,128)(2,1)} custom-call(s32[1]{0:T(128)} %bitcast.9.x_ref, s32[1]{0:T(128)} %bitcast.1.core_ref, bf16[2,8,64,384]{3,2,1,0:T(8,128)(2,1)S(1)} %collective-permute-done.5.refs_0_, bf16[64,24576]{1,0:T(8,128)(2,1)} %shard_map.92.refs_1_), custom_call_target="tpu_custom_call", output_to_operand_aliasing={{}: (3, {})} | custom-call | bytes 4000000 | tf_op jit(solution)/shard_map/pallas_call | solution.py:400
Async XLA Ops:
  7.2 74.1 %reduce-scatter.2.cloned.1.call-start = ((), (), s32[]{:S(2)}) async-start(), calls=%async_computation.5 | async-start | bytes 3538944 | tf_op jit(solution)/shard_map/reduce_scatter | solution.py:302
  9.4 14.9 %all-to-all-start = ((s32[8,16,128]{2,1,0:T(8,128)}), s32[8,16,128]{2,1,0:T(8,128)S(1)}, u32[]{:S(2)}, u32[]{:S(2)}) async-start(s32[8,16,128]{2,1,0:T(8,128)} %shard_map.87.ids_ref), calls=%async_computation.1 | async-start | bytes 131072 | tf_op jit(solution)/shard_map/all_to_all | solution.py:315
  17.1 7.2 %copy-start.2 = (bf16[4,64,64]{2,1,0:T(8,128)(2,1)S(1)}, bf16[4,64,64]{2,1,0:T(8,128)(2,1)}, u32[]{:S(2)}) copy-start(bf16[4,64,64]{2,1,0:T(8,128)(2,1)} %constant.20.clone.tab_hbm) | copy-start | bytes 98308
  23.4 18.6 %copy-start.1 = (s32[8,16,128]{2,1,0:T(8,128)S(1)}, s32[8,16,128]{2,1,0:T(8,128)}, u32[]{:S(2)}) copy-start(s32[8,16,128]{2,1,0:T(8,128)} %shard_map.87.ids_ref) | copy-start | bytes 196612
  23.4 81.9 %copy-start = (f32[1,64,3072]{2,1,0:T(8,128)S(1)}, f32[1,64,3072]{2,1,0:T(8,128)}, u32[]{:S(2)}) copy-start(f32[1,64,3072]{2,1,0:T(8,128)} %param.8) | copy-start | bytes 2359300
  23.4 81.9 %copy-start.3 = (bf16[256,512]{1,0:T(8,128)(2,1)S(1)}, bf16[256,512]{1,0:T(8,128)(2,1)}, u32[]{:S(2)}) copy-start(bf16[256,512]{1,0:T(8,128)(2,1)} %constant.19.clone.wide_hbm.wide_ref) | copy-start | bytes 786436
  23.4 81.9 %copy-start.5 = (f32[64,128]{1,0:T(8,128)S(1)}, f32[64,128]{1,0:T(8,128)}, u32[]{:S(2)}) copy-start(f32[64,128]{1,0:T(8,128)} %constant.21.clone.ct_ref) | copy-start | bytes 98308
  42.7 36.3 %all-to-all-start.2 = ((f32[96,1,384]{2,1,0:T(1,128)}), f32[96,1,384]{2,1,0:T(1,128)S(1)}, u32[]{:S(2)}, u32[]{:S(2)}) async-start(f32[96,1,384]{2,1,0:T(1,128)} %bitcast.7), calls=%async_computation.3 | async-start | bytes 294912 | tf_op jit(solution)/shard_map/all_to_all | solution.py:352
  96.7 18.4 %collective-permute-start = (bf16[8,64,384]{2,1,0:T(8,128)(2,1)S(1)}, bf16[8,64,384]{2,1,0:T(8,128)(2,1)S(1)}, u32[]{:S(2)}, u32[]{:S(2)}) collective-permute-start(bf16[8,64,384]{2,1,0:T(8,128)(2,1)S(1)} %all_to_all.21.refs_0_), channel_id=1, source_target_pairs={{0,384},{192,576},{384,0},{576,192},{1,385},{193,577},{385,1},{577... | collective-permute-start | bytes 1179656 | tf_op jit(solution)/shard_map/ppermute | solution.py:367
  99.5 17.5 %collective-permute-start.4 = (bf16[8,64,384]{2,1,0:T(8,128)(2,1)S(1)}, bf16[8,64,384]{2,1,0:T(8,128)(2,1)S(1)}, u32[]{:S(2)}, u32[]{:S(2)}) collective-permute-start(bf16[8,64,384]{2,1,0:T(8,128)(2,1)S(1)} %all_to_all.21.refs_0_), channel_id=1, source_target_pairs={{0,576},{192,0},{384,192},{576,384},{1,577},{193,1},{385,193},{577... | collective-permute-start | bytes 1179656 | tf_op jit(solution)/shard_map/ppermute | solution.py:367
  103.3 14.9 %collective-permute-start.3 = (bf16[8,64,384]{2,1,0:T(8,128)(2,1)S(1)}, bf16[8,64,384]{2,1,0:T(8,128)(2,1)S(1)}, u32[]{:S(2)}, u32[]{:S(2)}) collective-permute-start(bf16[8,64,384]{2,1,0:T(8,128)(2,1)S(1)} %all_to_all.21.refs_0_), channel_id=1, source_target_pairs={{0,192},{192,384},{384,576},{576,0},{1,193},{193,385},{385,577},{5... | collective-permute-start | bytes 1179656 | tf_op jit(solution)/shard_map/ppermute | solution.py:367
  105.3 1.0 copy-start.4
  110.0 8.4 %collective-permute-start.1 = (bf16[8,64,384]{2,1,0:T(8,128)(2,1)S(1)}, bf16[8,64,384]{2,1,0:T(8,128)(2,1)S(1)}, u32[]{:S(2)}, u32[]{:S(2)}) collective-permute-start(bf16[8,64,384]{2,1,0:T(8,128)(2,1)S(1)} %all_to_all.21.refs_0_), channel_id=1, source_target_pairs={{0,8},{8,0},{1,9},{9,1},{2,10},{10,2},{3,11},{11,3},{4,12},{12,4},... | collective-permute-start | bytes 1179656 | tf_op jit(solution)/shard_map/ppermute | solution.py:370
  115.1 3.6 %collective-permute-start.2 = (bf16[8,64,384]{2,1,0:T(8,128)(2,1)S(1)}, bf16[8,64,384]{2,1,0:T(8,128)(2,1)S(1)}, u32[]{:S(2)}, u32[]{:S(2)}) collective-permute-start(bf16[8,64,384]{2,1,0:T(8,128)(2,1)S(1)} %collective-permute-done.refs_1_), channel_id=1, source_target_pairs={{0,8},{8,0},{1,9},{9,1},{2,10},{10,2},{3,11},{11,3},{4,12},{12,4},... | collective-permute-start | bytes 1179656 | tf_op jit(solution)/shard_map/ppermute | solution.py:370
  118.7 5.9 %collective-permute-start.5 = (bf16[2,8,64,384]{3,2,1,0:T(8,128)(2,1)S(1)}, bf16[2,8,64,384]{3,2,1,0:T(8,128)(2,1)S(1)}, u32[]{:S(2)}, u32[]{:S(2)}) collective-permute-start(bf16[2,8,64,384]{3,2,1,0:T(8,128)(2,1)S(1)} %pad_maximum_fusion.refs_2_), channel_id=1, source_target_pairs={{0,8},{8,0},{1,9},{9,1},{2,10},{10,2},{3,11},{11,3},{4,12},{12,4},... | collective-permute-start | bytes 2359304 | tf_op jit(solution)/shard_map/ppermute | solution.py:370
Sparse Core Ops, SparseCore 0:
  11.1 57.5 reduce-scatter.1
where the time goes:
time: 133 us
  starting transfers between devices  48.8 us (37%)
  blocking collectives  28.8 us (22%)
  Pallas kernels  22.1 us (17%)
  waiting for transfers between devices  17.8 us (13%)
  between operations  14.3 us (11%)
    all_to_all x1, starting transfers between devices, on_device(): lax.all_to_all(sent.reshape(NX * peers, 1, 3 * LANES), ('x', 'z', 'core')...  21.7 us
    all_to_all x1, blocking collectives, on_device(): field = lax.all_to_all(field, 'leaf', 0, 0, tiled=True)  15.4 us
    all_to_all x1, waiting for transfers between devices, on_device(): lax.all_to_all(sent.reshape(NX * peers, 1, 3 * LANES), ('x', 'z', 'core')...  14.6 us
    all_to_all x1, blocking collectives, on_device(): got = lax.all_to_all(partial, 'leaf', 0, 0, tiled=True)  13.3 us
    ppermute x3, starting transfers between devices, across(): return lax.ppermute(a, 'core', [(0, 1), (1, 0)])  10.9 us
    ppermute x3, starting transfers between devices, along_x(): return lax.ppermute(field, 'x', [(i, (i + hops) % NX) for i in range(NX)])  8.57 us
    all_to_all x1, starting transfers between devices, on_device(): all_ids = lax.all_to_all(own_ids, 'leaf', 0, 0, tiled=True)  7.66 us
    pallas_call x1, Pallas kernels, on_device(): call(functools.partial(dense_kernel, leaves), jax.ShapeDtypeStruct((leave...  6.27 us
  transfers between devices with their start and end apart: 9, of which 4 were waited for; matrix products, arithmetic and copies ran while one was open for 0% of the time, Pallas kernels for 16%

commit v1 on v0

--- a/solution.py
+++ b/solution.py
@@ -375,6 +375,7 @@
     residual = call(
         functools.partial(residual_kernel, step),
         jax.ShapeDtypeStruct((SPAN, own_cols), F32),
+        vmem=57 * 1024 * 1024,
         grid=(rows // step,),
         in_specs=[
             pl.BlockSpec((SPAN, step * QUAD), lambda i: (0, i)),

time: 133 us -> 133 us (level)
  Pallas kernels: 22.1 us -> 23.5 us
    pallas_call x1, Pallas kernels: 3.7 us -> 5.1 us  [on_device(): call(functools.partial(residual_kernel, step), jax.ShapeDtypeStruct((SPAN...]
  transfers between devices with their start and end apart: 9 -> 9, of which waited for: 4 -> 4; matrix products, arithmetic and copies ran while one was open for 0% -> 0% of each run, Pallas kernels for 16% -> 17%
where the time goes in v1:
time: 133 us
  starting transfers between devices  48.7 us (37%)
  blocking collectives  28.3 us (21%)
  Pallas kernels  23.5 us (18%)
  waiting for transfers between devices  17.8 us (13%)
  between operations  14.2 us (11%)
    all_to_all x1, starting transfers between devices, on_device(): lax.all_to_all(sent.reshape(NX * peers, 1, 3 * LANES), ('x', 'z', 'core')...  21.9 us
    all_to_all x1, blocking collectives, on_device(): field = lax.all_to_all(field, 'leaf', 0, 0, tiled=True)  15.4 us
    all_to_all x1, waiting for transfers between devices, on_device(): lax.all_to_all(sent.reshape(NX * peers, 1, 3 * LANES), ('x', 'z', 'core')...  14.6 us
    all_to_all x1, blocking collectives, on_device(): got = lax.all_to_all(partial, 'leaf', 0, 0, tiled=True)  12.9 us
    ppermute x3, starting transfers between devices, across(): return lax.ppermute(a, 'core', [(0, 1), (1, 0)])  10.5 us
    ppermute x3, starting transfers between devices, along_x(): return lax.ppermute(field, 'x', [(i, (i + hops) % NX) for i in range(NX)])  8.57 us
    all_to_all x1, starting transfers between devices, on_device(): all_ids = lax.all_to_all(own_ids, 'leaf', 0, 0, tiled=True)  7.66 us
    pallas_call x1, Pallas kernels, on_device(): call(functools.partial(dense_kernel, leaves), jax.ShapeDtypeStruct((leave...  6.26 us
  transfers between devices with their start and end apart: 9, of which 4 were waited for; matrix products, arithmetic and copies ran while one was open for 0% of the time, Pallas kernels for 17%

profile of v1, /device:TPU:1, one launch (start us, length us, event | category | flops | bytes accessed | tf_op | source)
XLA Modules:
  0.0 132.7 jit_solution(7392297030918886833)
XLA Ops:
  7.2 0.0 reduce-scatter.2.cloned.1.call-start
  7.2 0.7 reduce-scatter.2.cloned.1.call-update
  7.9 1.5 %shard_map.87.ids_ref = s32[8,16,128]{2,1,0:T(8,128)} custom-call(s32[32,48]{1,0:T(8,128)} %bitcast.19, s32[1,48]{1,0:T(1,128)} %bitcast.20), custom_call_target="tpu_custom_call" | custom-call | tf_op jit(solution)/shard_map/pallas_call | solution.py:304
  9.4 7.7 %all-to-all-start = ((s32[8,16,128]{2,1,0:T(8,128)}), s32[8,16,128]{2,1,0:T(8,128)S(1)}, u32[]{:S(2)}, u32[]{:S(2)}) async-start(s32[8,16,128]{2,1,0:T(8,128)} %shard_map.87.ids_ref), calls=%async_computation.1 | async-start | bytes 131072 | tf_op jit(solution)/shard_map/all_to_all | solution.py:315
  17.1 0.0 copy-start.1
  17.1 6.3 %shard_map.86.f_hbm = f32[8,768,256]{2,1,0:T(8,128)} custom-call(s32[1]{0:T(128)} %bitcast.2.me_ref, bf16[64,24576]{1,0:T(8,128)(2,1)} %bitcast.14, f32[64,3072]{1,0:T(8,128)} %bitcast.15, bf16[256,512]{1,0:T(8,128)(2,1)} %constant.19.clone.wide_hbm.wide_ref), custom_call_target="tpu_custom_call" | custom-call | flops 2000000000 | bytes 16000000 | tf_op jit(solution)/shard_map/pallas_call | solution.py:317
  23.4 0.0 copy-start
  23.4 0.9 all-to-all-done.ids_hbm
  24.3 0.0 copy-done.1
  24.3 4.3 %shard_map.88 = f32[8,16,128]{2,1,0:T(8,128)S(1)} custom-call(f32[8,768,256]{2,1,0:T(8,128)} %shard_map.86.f_hbm, s32[8,16,128]{2,1,0:T(8,128)S(1)} %all-to-all-done.ids_hbm, bf16[4,64,64]{2,1,0:T(8,128)(2,1)S(1)} %copy-done.1), custom_call_target="tpu_custom_call" | custom-call | tf_op jit(solution)/shard_map/pallas_call | solution.py:334
  28.6 12.9 %all_to_all.20.got_ref = f32[8,16,128]{2,1,0:T(8,128)S(1)} all-to-all(f32[8,16,128]{2,1,0:T(8,128)S(1)} %shard_map.88), channel_id=1, replica_groups=mesh['x'=4,'z'=12,'core'=2,'leaf'=8] {'leaf'}, dimensions={0} | all-to-all | bytes 131072 | tf_op jit(solution)/shard_map/all_to_all | solution.py:346
  41.5 0.0 copy-done
  41.5 0.8 shard_map.89
  42.3 21.9 %all-to-all-start.2 = ((f32[96,1,384]{2,1,0:T(1,128)}), f32[96,1,384]{2,1,0:T(1,128)S(1)}, u32[]{:S(2)}, u32[]{:S(2)}) async-start(f32[96,1,384]{2,1,0:T(1,128)} %bitcast.7), calls=%async_computation.3 | async-start | bytes 294912 | tf_op jit(solution)/shard_map/all_to_all | solution.py:352
  64.2 14.6 %all-to-all-done.2.got_ref = f32[96,1,384]{2,1,0:T(1,128)S(1)} async-done(((f32[96,1,384]{2,1,0:T(1,128)}), f32[96,1,384]{2,1,0:T(1,128)S(1)}, u32[]{:S(2)}, u32[]{:S(2)}) %all-to-all-start.2) | async-done | bytes 147488 | tf_op jit(solution)/shard_map/all_to_all | solution.py:352
  78.8 2.2 %shard_map.90 = bf16[8,64,384]{2,1,0:T(8,128)(2,1)S(1)} custom-call(s32[1]{0:T(128)} %bitcast.1.core_ref, f32[96,1,384]{2,1,0:T(1,128)S(1)} %all-to-all-done.2.got_ref, bf16[4,64,64]{2,1,0:T(8,128)(2,1)S(1)} %copy-done.1), custom_call_target="tpu_custom_call" | custom-call | tf_op jit(solution)/shard_map/pallas_call | solution.py:357
  81.0 0.0 reduce-scatter.2.cloned.1.call-done.sum_ref
  81.1 15.4 %all_to_all.21.refs_0_ = bf16[8,64,384]{2,1,0:T(8,128)(2,1)S(1)} all-to-all(bf16[8,64,384]{2,1,0:T(8,128)(2,1)S(1)} %shard_map.90), channel_id=1, replica_groups=mesh['x'=4,'z'=12,'core'=2,'leaf'=8] {'leaf'}, dimensions={0} | all-to-all | bytes 786432 | tf_op jit(solution)/shard_map/all_to_all | solution.py:364
  96.5 2.8 %collective-permute-start = (bf16[8,64,384]{2,1,0:T(8,128)(2,1)S(1)}, bf16[8,64,384]{2,1,0:T(8,128)(2,1)S(1)}, u32[]{:S(2)}, u32[]{:S(2)}) collective-permute-start(bf16[8,64,384]{2,1,0:T(8,128)(2,1)S(1)} %all_to_all.21.refs_0_), channel_id=1, source_target_pairs={{0,384},{192,576},{384,0},{576,192},{1,385},{193,577},{385,1},{577... | collective-permute-start | bytes 1179656 | tf_op jit(solution)/shard_map/ppermute | solution.py:367
  99.3 3.9 %collective-permute-start.4 = (bf16[8,64,384]{2,1,0:T(8,128)(2,1)S(1)}, bf16[8,64,384]{2,1,0:T(8,128)(2,1)S(1)}, u32[]{:S(2)}, u32[]{:S(2)}) collective-permute-start(bf16[8,64,384]{2,1,0:T(8,128)(2,1)S(1)} %all_to_all.21.refs_0_), channel_id=1, source_target_pairs={{0,576},{192,0},{384,192},{576,384},{1,577},{193,1},{385,193},{577... | collective-permute-start | bytes 1179656 | tf_op jit(solution)/shard_map/ppermute | solution.py:367
  103.2 1.9 %collective-permute-start.3 = (bf16[8,64,384]{2,1,0:T(8,128)(2,1)S(1)}, bf16[8,64,384]{2,1,0:T(8,128)(2,1)S(1)}, u32[]{:S(2)}, u32[]{:S(2)}) collective-permute-start(bf16[8,64,384]{2,1,0:T(8,128)(2,1)S(1)} %all_to_all.21.refs_0_), channel_id=1, source_target_pairs={{0,192},{192,384},{384,576},{576,0},{1,193},{193,385},{385,577},{5... | collective-permute-start | bytes 1179656 | tf_op jit(solution)/shard_map/ppermute | solution.py:367
  105.1 5.1 %shard_map.91 = f32[64,3072]{1,0:T(8,128)} custom-call(bf16[64,3072]{1,0:T(8,128)(2,1)} %reduce-scatter.2.cloned.1.call-done.sum_ref, f32[64,3072]{1,0:T(8,128)} %bitcast.16, s32[8,16,128]{2,1,0:T(8,128)} %shard_map.87.ids_ref, bf16[256,512]{1,0:T(8,128)(2,1)} %constant.19.clone.wide_hbm.wide_ref, f32[64,128]{1,0:T(8,128)} %constant.21.clone.ct_ref), custom_call_target="tpu_custom_call" | custom-call | flops 1000000000 | bytes 16000000 | tf_op jit(solution)/shard_map/pallas_call | solution.py:375
  110.2 5.1 %collective-permute-start.1 = (bf16[8,64,384]{2,1,0:T(8,128)(2,1)S(1)}, bf16[8,64,384]{2,1,0:T(8,128)(2,1)S(1)}, u32[]{:S(2)}, u32[]{:S(2)}) collective-permute-start(bf16[8,64,384]{2,1,0:T(8,128)(2,1)S(1)} %all_to_all.21.refs_0_), channel_id=1, source_target_pairs={{0,8},{8,0},{1,9},{9,1},{2,10},{10,2},{3,11},{11,3},{4,12},{12,4},... | collective-permute-start | bytes 1179656 | tf_op jit(solution)/shard_map/ppermute | solution.py:370
  115.3 0.0 collective-permute-done.refs_1_
  115.3 1.9 %collective-permute-start.2 = (bf16[8,64,384]{2,1,0:T(8,128)(2,1)S(1)}, bf16[8,64,384]{2,1,0:T(8,128)(2,1)S(1)}, u32[]{:S(2)}, u32[]{:S(2)}) collective-permute-start(bf16[8,64,384]{2,1,0:T(8,128)(2,1)S(1)} %collective-permute-done.refs_1_), channel_id=1, source_target_pairs={{0,8},{8,0},{1,9},{9,1},{2,10},{10,2},{3,11},{11,3},{4,12},{12,4},... | collective-permute-start | bytes 1179656 | tf_op jit(solution)/shard_map/ppermute | solution.py:370
  117.2 0.0 collective-permute-done.4
  117.2 0.9 collective-permute-done.3
  118.1 0.1 pad_maximum_fusion.refs_2_
  118.2 0.0 collective-permute-done.1.refs_3_
  118.2 0.7 collective-permute-done.2.refs_4_
  118.9 3.5 %collective-permute-start.5 = (bf16[2,8,64,384]{3,2,1,0:T(8,128)(2,1)S(1)}, bf16[2,8,64,384]{3,2,1,0:T(8,128)(2,1)S(1)}, u32[]{:S(2)}, u32[]{:S(2)}) collective-permute-start(bf16[2,8,64,384]{3,2,1,0:T(8,128)(2,1)S(1)} %pad_maximum_fusion.refs_2_), channel_id=1, source_target_pairs={{0,8},{8,0},{1,9},{9,1},{2,10},{10,2},{3,11},{11,3},{4,12},{12,4},... | collective-permute-start | bytes 2359304 | tf_op jit(solution)/shard_map/ppermute | solution.py:370
  122.4 1.9 %shard_map.92.refs_1_ = bf16[64,24576]{1,0:T(8,128)(2,1)} custom-call(s32[1]{0:T(128)} %bitcast.9.x_ref, s32[1]{0:T(128)} %bitcast.1.core_ref, bf16[8,64,384]{2,1,0:T(8,128)(2,1)S(1)} %all_to_all.21.refs_0_, bf16[8,64,384]{2,1,0:T(8,128)(2,1)S(1)} %collective-permute-done.refs_1_, bf16[2,8,64,384]{3,2,1,0:T(8,128)(2,1)S(1)} %pad_maximum_fusion.refs_2_, ...), custom_call_target="tpu_custom_call" | custom-call | bytes 4000000 | tf_op jit(solution)/shard_map/pallas_call | solution.py:401
  124.4 0.0 collective-permute-done.5.refs_0_
  124.4 1.4 %shard_map.93 = bf16[64,24576]{1,0:T(8,128)(2,1)} custom-call(s32[1]{0:T(128)} %bitcast.9.x_ref, s32[1]{0:T(128)} %bitcast.1.core_ref, bf16[2,8,64,384]{3,2,1,0:T(8,128)(2,1)S(1)} %collective-permute-done.5.refs_0_, bf16[64,24576]{1,0:T(8,128)(2,1)} %shard_map.92.refs_1_), custom_call_target="tpu_custom_call", output_to_operand_aliasing={{}: (3, {})} | custom-call | bytes 4000000 | tf_op jit(solution)/shard_map/pallas_call | solution.py:401
Async XLA Ops:
  7.2 73.9 %reduce-scatter.2.cloned.1.call-start = ((), (), s32[]{:S(2)}) async-start(), calls=%async_computation.5 | async-start | bytes 3538944 | tf_op jit(solution)/shard_map/reduce_scatter | solution.py:302
  9.4 14.9 %all-to-all-start = ((s32[8,16,128]{2,1,0:T(8,128)}), s32[8,16,128]{2,1,0:T(8,128)S(1)}, u32[]{:S(2)}, u32[]{:S(2)}) async-start(s32[8,16,128]{2,1,0:T(8,128)} %shard_map.87.ids_ref), calls=%async_computation.1 | async-start | bytes 131072 | tf_op jit(solution)/shard_map/all_to_all | solution.py:315
  17.1 7.2 %copy-start.1 = (bf16[4,64,64]{2,1,0:T(8,128)(2,1)S(1)}, bf16[4,64,64]{2,1,0:T(8,128)(2,1)}, u32[]{:S(2)}) copy-start(bf16[4,64,64]{2,1,0:T(8,128)(2,1)} %constant.20.clone.tab_hbm) | copy-start | bytes 98308
  23.4 18.1 %copy-start = (s32[8,16,128]{2,1,0:T(8,128)S(1)}, s32[8,16,128]{2,1,0:T(8,128)}, u32[]{:S(2)}) copy-start(s32[8,16,128]{2,1,0:T(8,128)} %shard_map.87.ids_ref) | copy-start | bytes 196612
  42.3 36.5 %all-to-all-start.2 = ((f32[96,1,384]{2,1,0:T(1,128)}), f32[96,1,384]{2,1,0:T(1,128)S(1)}, u32[]{:S(2)}, u32[]{:S(2)}) async-start(f32[96,1,384]{2,1,0:T(1,128)} %bitcast.7), calls=%async_computation.3 | async-start | bytes 294912 | tf_op jit(solution)/shard_map/all_to_all | solution.py:352
  96.5 18.8 %collective-permute-start = (bf16[8,64,384]{2,1,0:T(8,128)(2,1)S(1)}, bf16[8,64,384]{2,1,0:T(8,128)(2,1)S(1)}, u32[]{:S(2)}, u32[]{:S(2)}) collective-permute-start(bf16[8,64,384]{2,1,0:T(8,128)(2,1)S(1)} %all_to_all.21.refs_0_), channel_id=1, source_target_pairs={{0,384},{192,576},{384,0},{576,192},{1,385},{193,577},{385,1},{577... | collective-permute-start | bytes 1179656 | tf_op jit(solution)/shard_map/ppermute | solution.py:367
  99.3 17.9 %collective-permute-start.4 = (bf16[8,64,384]{2,1,0:T(8,128)(2,1)S(1)}, bf16[8,64,384]{2,1,0:T(8,128)(2,1)S(1)}, u32[]{:S(2)}, u32[]{:S(2)}) collective-permute-start(bf16[8,64,384]{2,1,0:T(8,128)(2,1)S(1)} %all_to_all.21.refs_0_), channel_id=1, source_target_pairs={{0,576},{192,0},{384,192},{576,384},{1,577},{193,1},{385,193},{577... | collective-permute-start | bytes 1179656 | tf_op jit(solution)/shard_map/ppermute | solution.py:367
  103.2 14.9 %collective-permute-start.3 = (bf16[8,64,384]{2,1,0:T(8,128)(2,1)S(1)}, bf16[8,64,384]{2,1,0:T(8,128)(2,1)S(1)}, u32[]{:S(2)}, u32[]{:S(2)}) collective-permute-start(bf16[8,64,384]{2,1,0:T(8,128)(2,1)S(1)} %all_to_all.21.refs_0_), channel_id=1, source_target_pairs={{0,192},{192,384},{384,576},{576,0},{1,193},{193,385},{385,577},{5... | collective-permute-start | bytes 1179656 | tf_op jit(solution)/shard_map/ppermute | solution.py:367
  110.2 8.0 %collective-permute-start.1 = (bf16[8,64,384]{2,1,0:T(8,128)(2,1)S(1)}, bf16[8,64,384]{2,1,0:T(8,128)(2,1)S(1)}, u32[]{:S(2)}, u32[]{:S(2)}) collective-permute-start(bf16[8,64,384]{2,1,0:T(8,128)(2,1)S(1)} %all_to_all.21.refs_0_), channel_id=1, source_target_pairs={{0,8},{8,0},{1,9},{9,1},{2,10},{10,2},{3,11},{11,3},{4,12},{12,4},... | collective-permute-start | bytes 1179656 | tf_op jit(solution)/shard_map/ppermute | solution.py:370
  115.3 3.6 %collective-permute-start.2 = (bf16[8,64,384]{2,1,0:T(8,128)(2,1)S(1)}, bf16[8,64,384]{2,1,0:T(8,128)(2,1)S(1)}, u32[]{:S(2)}, u32[]{:S(2)}) collective-permute-start(bf16[8,64,384]{2,1,0:T(8,128)(2,1)S(1)} %collective-permute-done.refs_1_), channel_id=1, source_target_pairs={{0,8},{8,0},{1,9},{9,1},{2,10},{10,2},{3,11},{11,3},{4,12},{12,4},... | collective-permute-start | bytes 1179656 | tf_op jit(solution)/shard_map/ppermute | solution.py:370
  118.9 5.5 %collective-permute-start.5 = (bf16[2,8,64,384]{3,2,1,0:T(8,128)(2,1)S(1)}, bf16[2,8,64,384]{3,2,1,0:T(8,128)(2,1)S(1)}, u32[]{:S(2)}, u32[]{:S(2)}) collective-permute-start(bf16[2,8,64,384]{3,2,1,0:T(8,128)(2,1)S(1)} %pad_maximum_fusion.refs_2_), channel_id=1, source_target_pairs={{0,8},{8,0},{1,9},{9,1},{2,10},{10,2},{3,11},{11,3},{4,12},{12,4},... | collective-permute-start | bytes 2359304 | tf_op jit(solution)/shard_map/ppermute | solution.py:370
Sparse Core Ops, SparseCore 0:
  11.1 58.1 reduce-scatter.1
